TPU v7x, 512 devices: a whole 4x8x8 slice. The times are simulated.
512 devices in a mesh: hour: 64 (over z_hi, y, core), bus: 8 (over x, z_lo).
Axes of the slice: x: 4, y: 8, z: 8 (z_hi: 4, z_lo: 2; z = z_hi * 2 + z_lo), core: 2. Of those that a mesh axis runs over, the one named last changes fastest.
Arguments:
- line_sensitivity: float32 [2000, 3072], P('bus'), may hold values from -0.125 to 0.125
- demand: float32 [2000, 8192], P('bus', 'hour'), may hold values from 0.05 to 1
- unit_cost: float32 [2000, 8192], P('bus', 'hour'), may hold values from 0.1 to 2
- output_limit: float32 [2000], P('bus'), may hold values from 0.2 to 2
- output_start: float32 [2000, 8192], P('bus', 'hour'), may hold values from 0 to 1
- line_limit: float32 [3072], replicated, may hold values from 0.1 to 1
- line_dual: float32 [3072, 8192], P('bus', 'hour'), may hold values from -3 to 3
- storage_bus: int32 [2000], P('bus'), may hold values from 0 to 1999, as said below
- charge_limit: float32 [2000], P('bus'), may hold values from 0.05 to 0.5
- charge_start: float32 [2000, 8192], P('bus', 'hour'), may hold values from -0.2 to 0.2
- level_start: float32 [2000], P('bus'), may hold values from 1 to 6
- level_limit: float32 [2000], P('bus'), may hold values from 3 to 30
- level_dual: float32 [2000, 8192], P('bus', 'hour'), may hold values from -0.2 to 0.2
- balance_dual: float32 [8192], P('hour'), may hold values from -3 to 3
Outputs:
- generation: float32 [2000, 8192], P('bus', 'hour')
- charging: float32 [2000, 8192], P('bus', 'hour')
- storage_level: float32 [2000, 8192], P('bus', 'hour')
- line_dual_next: float32 [3072, 8192], P('bus', 'hour')
- level_dual_next: float32 [2000, 8192], P('bus', 'hour')
- balance_dual_next: float32 [8192], P('hour')
Inputs may be any that keep to these rules, and one draw needn't show every extreme that they name: `storage_bus`: storage s is connected to a bus b with b // 250 equal to s // 250; storage 0 is at bus 0 and storage 2000 - 1 at bus 2000 - 1.
All inputs are finite; a program needn't handle non-finite values.
Results may differ from a plain program's by a relative error of at most 0.00011.
Values sent between devices are 32-bit elements; how exact they have to be, the bound alone decides.
A program may use at most 64 MiB of HBM per device.

v0:
```python
import jax
import jax.numpy as jnp
from jax import lax
from jax.sharding import PartitionSpec as P

B = 2000
S = 2000
ITERS = 2


def prefix(value, axis, combine, identity, reverse):
    devices, index = (lax.axis_size(axis), lax.axis_index(axis))
    everything = lax.all_gather(value, axis)
    start = jnp.broadcast_to(jnp.asarray(identity, value.dtype), value.shape)

    def hop(k, before):
        at = devices - 1 - k if reverse else k
        reached = at > index if reverse else at < index
        new = combine(before, everything[at])
        return jnp.where(reached, new, before)

    return lax.fori_loop(0, devices, hop, start)


def combine_sum(earlier, later):
    return earlier + later


def level_of(charge_bar, level_start, zeros_store):
    carried = prefix(jnp.sum(charge_bar, axis=1), "hour", combine_sum, zeros_store, False)
    return level_start[:, None] + carried[:, None] + jnp.cumsum(charge_bar, axis=1)


def later_of(level_now, zeros_store):
    beyond = prefix(jnp.sum(level_now, axis=1), "hour", combine_sum, zeros_store, True)
    return beyond[:, None] + jnp.flip(jnp.cumsum(jnp.flip(level_now, 1), axis=1), 1)


def flow_update(line_sensitivity, injection):
    column_sum = jnp.sum(injection, axis=0)
    partial_value = lax.dot_general(
        line_sensitivity,
        injection,
        (((0,), (0,)), ((), ())),
        precision=lax.Precision.HIGHEST,
        preferred_element_type=jnp.float32,
    )
    flows, balance = lax.psum((partial_value, column_sum), "bus")
    return (flows, balance)


def body(
    line_sensitivity,
    demand,
    unit_cost,
    output_limit,
    output_start,
    line_limit,
    line_dual,
    storage_bus,
    charge_limit,
    charge_start,
    level_start,
    level_limit,
    level_dual,
    balance_dual,
):
    hours_dev = demand.shape[1]
    buses_dev = line_sensitivity.shape[0]
    lines_dev = line_dual.shape[0]
    stores_dev = charge_start.shape[0]
    hour_pos = (lax.axis_index("hour") * hours_dev + lax.iota(jnp.int32, hours_dev)).astype(
        jnp.float32
    )
    all_hours = float(hours_dev * lax.axis_size("hour"))
    step_charge = 1.0 / (all_hours - hour_pos + 4.0)
    local_bus = storage_bus - lax.axis_index("bus") * buses_dev
    line_base = lax.axis_index("bus") * lines_dev
    zeros_store = jnp.zeros((stores_dev,), jnp.float32)
    line_now = lax.all_gather(line_dual, "bus", axis=0, tiled=True)
    generation = output_start
    charging = charge_start
    level_now = level_dual
    balance_now = balance_dual
    storage_level = charge_start
    for iteration in range(ITERS):
        adjoint = jnp.dot(
            line_sensitivity,
            line_now,
            precision=lax.Precision.HIGHEST,
            preferred_element_type=jnp.float32,
        )
        later = later_of(level_now, zeros_store)
        output_new = jnp.clip(
            generation - 0.25 * (unit_cost + adjoint + balance_now[None, :]),
            0.0,
            output_limit[:, None],
        )
        charge_grad = later - jnp.take(adjoint, local_bus, axis=0) - balance_now[None, :]
        charge_new = jnp.clip(
            charging - step_charge[None, :] * charge_grad,
            -charge_limit[:, None],
            charge_limit[:, None],
        )
        output_bar = 2.0 * output_new - generation
        charge_bar = 2.0 * charge_new - charging
        injection = (
            output_bar - demand - jax.ops.segment_sum(charge_bar, local_bus, num_segments=buses_dev)
        )
        flows, balance = flow_update(line_sensitivity, injection)
        storage_level = level_of(charge_bar, level_start, zeros_store)
        raised = 4.0 * line_now + flows
        line_now = 0.25 * (raised - jnp.clip(raised, -line_limit[:, None], line_limit[:, None]))
        raised_level = 4.0 * level_now + storage_level
        level_now = 0.25 * (raised_level - jnp.clip(raised_level, 0.0, level_limit[:, None]))
        balance_now = balance_now + balance / float(B + S)
        generation = output_new
        charging = charge_new
    line_out = lax.dynamic_slice_in_dim(line_now, line_base, lines_dev, 0)
    return (generation, charging, storage_level, line_out, level_now, balance_now)


def solution(mesh):
    placed = (
        P("bus", None),
        P("bus", "hour"),
        P("bus", "hour"),
        P("bus"),
        P("bus", "hour"),
        P(),
        P("bus", "hour"),
        P("bus"),
        P("bus"),
        P("bus", "hour"),
        P("bus"),
        P("bus"),
        P("bus", "hour"),
        P("hour"),
    )
    return jax.shard_map(
        body,
        mesh=mesh,
        in_specs=placed,
        out_specs=(
            P("bus", "hour"),
            P("bus", "hour"),
            P("bus", "hour"),
            P("bus", "hour"),
            P("bus", "hour"),
            P("hour"),
        ),
        check_vma=False,
    )
```

profile of v0, /device:TPU:1, one launch (start us, length us, event | category | flops | bytes accessed | tf_op | source)
XLA Modules:
  0.0 1475.9 jit_solution(10019087947950708436)
XLA Ops:
  7.3 1.9 copy.20
  10.3 1.3 dynamic-slice
  12.5 282.8 %all-reduce = f32[16000]{0:T(1024)S(1)} all-reduce(f32[16000]{0:T(1024)S(1)} %dynamic-update-slice), channel_id=2, replica_groups=mesh['hour'=64,'bus'=8] {'hour'}, use_global_device_ids=true, to_apply=%add | all-reduce | flops 16000 | bytes 128000
  295.5 4.0 while.60
  305.4 4.0 fusion.27
  309.4 1.6 gather_fusion
  311.0 2.5 fusion.24
  313.6 1.7 copy.24
  315.3 2.4 scatter_custom_fusion
  317.6 2.3 fusion.26
  320.0 2.9 convolution_bitcast_fusion.1
  324.6 1.7 copy.25
  327.1 276.3 %all-reduce.1 = f32[16000]{0:T(1024)S(1)} all-reduce(f32[16000]{0:T(1024)S(1)} %dynamic-update-slice.1), channel_id=3, replica_groups=mesh['hour'=64,'bus'=8] {'hour'}, use_global_device_ids=true, to_apply=%add.1 | all-reduce | flops 16000 | bytes 128000
  604.3 123.9 %while.61 = (s32[]{:T(128)}, f32[250]{0:T(256)}, s32[]{:T(128)}, f32[64,250]{1,0:T(8,128)}, s32[]{:T(128)}, /*index=5*/s32[]{:T(128)}) while((s32[]{:T(128)}, f32[250]{0:T(256)}, s32[]{:T(128)}, f32[64,250]{1,0:T(8,128)}, s32[]{:T(128)}, /*index=5*/s32[]{:T(128)}) %tuple.149), condition=%wide.region_10.12_spmd.clone, body=%wide.region_9.11_spmd.clone.sunk | while | flops 754 | bytes 5101 | solution.py:22
  610.2 1.2 add_select_fusion.9
  612.1 1.2 add_select_fusion.9
  614.1 1.2 add_select_fusion.9
  619.9 1.2 add_select_fusion.9
  621.9 1.2 add_select_fusion.9
  629.7 1.2 add_select_fusion.9
  631.6 1.2 add_select_fusion.9
  637.4 1.2 add_select_fusion.9
  639.4 1.2 add_select_fusion.9
  641.3 1.2 add_select_fusion.9
  647.2 1.2 add_select_fusion.9
  649.1 1.2 add_select_fusion.9
  651.1 1.2 add_select_fusion.9
  656.9 1.2 add_select_fusion.9
  658.9 1.2 add_select_fusion.9
  666.6 1.2 add_select_fusion.9
  728.9 1.7 multiply_reduce_fusion
  731.5 274.9 %all-reduce.2 = f32[16000]{0:T(1024)S(1)} all-reduce(f32[16000]{0:T(1024)S(1)} %dynamic-update-slice.2), channel_id=4, replica_groups=mesh['hour'=64,'bus'=8] {'hour'}, use_global_device_ids=true, to_apply=%add.2 | all-reduce | flops 16000 | bytes 128000
  1007.2 47.0 %while.62 = (s32[]{:T(128)}, f32[250]{0:T(256)S(1)}, s32[]{:T(128)}, f32[64,250]{1,0:T(8,128)}, s32[]{:T(128)}, /*index=5*/s32[]{:T(128)}, s32[]{:T(128)}, s32[]{:T(128)}) while((s32[]{:T(128)}, f32[250]{0:T(256)S(1)}, s32[]{:T(128)}, f32[64,250]{1,0:T(8,128)}, s32[]{:T(128)}, /*index=5*/s32[]{:T(128)}, s32[]{:T(128)}, ...), condition=%wide.region_14.16_spmd.clone, body=%wide.region_13.15_spmd.clone.sunk | while | flops 758 | bytes 5163 | solution.py:22
  1058.5 1.6 rev.16
  1060.2 14.9 %psum.29 = f32[128]{0:T(128)S(1)} all-reduce(f32[128]{0:T(128)} %get-tuple-element.500), channel_id=1, replica_groups=mesh['hour'=64,'bus'=8] {'bus'}, use_global_device_ids=true, to_apply=%region_7.9 | all-reduce | flops 128 | bytes 1024 | tf_op jit(solution)/shard_map/psum | solution.py:48
  1076.4 2.1 minimum_subtract_fusion
  1079.7 2.6 fusion.2
  1082.3 1.5 gather_fusion.1
  1083.8 2.5 fusion.22
  1086.9 1.5 dynamic-update-slice.3
  1088.4 278.7 %all-reduce.3 = f32[16000]{0:T(1024)} all-reduce(f32[16000]{0:T(1024)} %dynamic-update-slice.3), channel_id=5, replica_groups=mesh['hour'=64,'bus'=8] {'hour'}, use_global_device_ids=true, to_apply=%add.3 | all-reduce | flops 16000 | bytes 128000
  1367.1 1.7 reshape.75
  1368.8 2.4 scatter_custom_fusion.1
  1371.2 2.3 fusion.21
  1373.5 2.9 convolution_bitcast_fusion
  1377.1 46.6 %while.63 = (s32[]{:T(128)}, f32[250]{0:T(256)S(1)}, s32[]{:T(128)}, f32[64,250]{1,0:T(8,128)}, s32[]{:T(128)}, /*index=5*/s32[]{:T(128)}) while((s32[]{:T(128)}, f32[250]{0:T(256)S(1)}, s32[]{:T(128)}, f32[64,250]{1,0:T(8,128)}, s32[]{:T(128)}, /*index=5*/s32[]{:T(128)}) %tuple.164), condition=%wide.region_18.20_spmd.clone, body=%wide.region_17.19_spmd.clone.sunk | while | flops 754 | bytes 5101 | solution.py:22
  1424.8 12.7 psum.31
  1439.4 28.0 %all-reduce.9.cloned.1.call-done = f32[3072,128]{0,1:T(8,128)} async-done(((f32[3072,128]{0,1:T(8,128)}), f32[3072,128]{0,1:T(8,128)}) %all-reduce.9.cloned.1.call-update) | async-done | bytes 1572880 | tf_op jit(solution)/shard_map/psum | solution.py:48
  (588 shorter events, 223.5 us)
Async XLA Ops:
  7.2 298.2 %copy-start = (f32[250,3072]{1,0:T(8,128)S(1)}, f32[250,3072]{1,0:T(8,128)}, u32[]{:S(2)}) copy-start(f32[250,3072]{1,0:T(8,128)} %param.24) | copy-start | bytes 9216004
  7.2 294.6 %copy-start.11 = (f32[250]{0:T(256)S(1)}, f32[250]{0:T(256)}, u32[]{:S(2)}) copy-start(f32[250]{0:T(256)} %param.32) | copy-start | bytes 3004
  7.2 295.1 %copy-start.7 = (f32[3072]{0:T(1024)S(1)}, f32[3072]{0:T(1024)}, u32[]{:S(2)}) copy-start(f32[3072]{0:T(1024)} %param.29) | copy-start | bytes 36868
  7.2 297.1 %copy-start.19 = (s32[250]{0:T(256)S(1)}, s32[250]{0:T(256)}, u32[]{:S(2)}) copy-start(s32[250]{0:T(256)} %param.31) | copy-start | bytes 3004
  7.2 298.2 %all-gather.6.cloned.1.call-start = ((), (), s32[]{:S(2)}) async-start(), calls=%async_computation | async-start | bytes 1769472 | tf_op jit(solution)/shard_map/all_gather | solution.py:80
  9.2 1067.2 %all-reduce.7.cloned.1.call-start = ((), (), s32[]{:S(2)}) async-start(), calls=%async_computation.1 | async-start | bytes 3145728 | tf_op jit(solution)/shard_map/psum | solution.py:48
  299.5 1.0 copy-start.9
  302.3 3.0 copy-start.8
  304.8 0.6 copy-start.18
  309.4 8.2 copy-start.3
  309.4 8.2 copy-start.4
  322.9 0.9 copy-start.5
  322.9 406.0 %copy-start.2 = (f32[250,128]{1,0:T(8,128)S(1)}, f32[250,128]{1,0:T(8,128)}, u32[]{:S(2)}) copy-start(f32[250,128]{1,0:T(8,128)} %param.36) | copy-start | bytes 384004
  322.9 1144.6 %all-reduce.9.cloned.1.call-start = ((), (), s32[]{:S(2)}) async-start(), calls=%async_computation.2 | async-start | bytes 3145728 | tf_op jit(solution)/shard_map/psum | solution.py:48
  1078.5 1.2 copy-start.1
  1079.7 4.1 copy-start.12
  1079.7 4.1 copy-start.13
  1079.7 4.1 copy-start.16
  1376.4 0.7 copy-start.10
  1376.4 47.3 %copy-start.6 = (f32[250,128]{1,0:T(8,128)S(1)}, f32[250,128]{1,0:T(8,128)}, u32[]{:S(2)}) copy-start(f32[250,128]{1,0:T(8,128)} %get-tuple-element.493) | copy-start | bytes 384004
  1376.4 62.2 %copy-start.17 = (f32[250]{0:T(256)S(1)}, f32[250]{0:T(256)}, u32[]{:S(2)}) copy-start(f32[250]{0:T(256)} %param.35) | copy-start | bytes 3004
  1376.4 91.1 %copy-start.14 = (f32[384]{0:T(512)S(1)}, f32[384]{0:T(512)}, u32[]{:S(2)}) copy-start(f32[384]{0:T(512)} %dynamic-slice.5) | copy-start | bytes 4612
  1376.4 91.1 %copy-start.15 = (f32[384]{0:T(512)S(1)}, f32[384]{0:T(512)}, u32[]{:S(2)}) copy-start(f32[384]{0:T(512)} %dynamic-slice.4) | copy-start | bytes 4612
Sparse Core Ops, SparseCore 0:
  10.7 52.3 all-gather.5
  323.1 92.4 all-reduce.6
  1376.6 90.8 all-reduce.8
where the time goes:
time: 1490 us; the launch traced here: 1480 us
  blocking collectives  1140 us (77%)
  local copies, waits for them, and re-layouts  164 us (11%)
  other arithmetic  112 us (8%)
  waiting for transfers between devices  28.1 us (2%)
    unnamed x4, blocking collectives  1110 us
    dynamic_slice x256, local copies, waits for them, and re-layouts, hop(): new = combine(before, everything[at])  136 us
    select_n x256, other arithmetic, hop(): return jnp.where(reached, new, before)  81.4 us
  transfers between devices with their start and end apart: 3, of which 1 were waited for; matrix products, arithmetic and copies ran while one was open for 17% of the time, Pallas kernels for 0%

commit v1 on v0

v1 whole, which is shorter than its diff:
```python
import jax
import jax.numpy as jnp
from jax import lax
from jax.experimental import pallas as pl
from jax.experimental.pallas import tpu as pltpu
from jax.sharding import PartitionSpec as P

B = 2000
S = 2000
ITERS = 2
HOURS = 8192
NB = 250
NP = 256
HD = 128
LD = 384
NL = 3072
NX = 4
GROUP = 8
ROW = 8
MESH = pl.DeviceIdType.MESH
HIGHEST = lax.Precision.HIGHEST
F32 = jnp.float32
BF16 = jnp.bfloat16
PEERS = ((2, 1), (1, 1), (3, 1), (2, 0), (1, 0), (3, 0), (0, 1))
ARRAYS = 14


def dot(a, b, dims, precision=None):
    return lax.dot_general(a, b, (dims, ((), ())), precision=precision, preferred_element_type=F32)


def halves(value):
    high = value.astype(BF16)
    return high, (value - high.astype(F32)).astype(BF16)


class Place:
    def __init__(self):
        self.hour = lax.axis_index("hour")
        self.bus = lax.axis_index("bus")
        self.x = self.bus // 2
        self.z = lax.rem(self.bus, 2)
        self.member = lax.rem(self.hour, GROUP)
        self.group = self.hour // GROUP

    def block(self, dx, dz):
        return lax.rem(self.x + dx + NX, NX) * 2 + lax.rem(self.z + dz, 2)

    def bus_peer(self, dx, dz):
        return (self.hour, self.block(dx, dz))

    def member_peer(self, d):
        return (self.group * GROUP + lax.rem(self.member + d, GROUP), self.bus)

    def group_peer(self, d):
        return (lax.rem(self.group + d, GROUP) * GROUP + self.member, self.bus)


class Sends:
    def __init__(self):
        self.all = []

    def start(self, src, dst, send_sem, recv_sem, device):
        copy = pltpu.make_async_remote_copy(
            src_ref=src, dst_ref=dst, send_sem=send_sem, recv_sem=recv_sem, device_id=device, device_id_type=MESH
        )
        copy.start()
        self.all.append(copy)

    def finish(self):
        for copy in self.all:
            copy.wait_send()


def arrived(ref, send_sem, recv_sem, device):
    pltpu.make_async_remote_copy(
        src_ref=ref, dst_ref=ref, send_sem=send_sem, recv_sem=recv_sem, device_id=device, device_id_type=MESH
    ).wait_recv()


class Gather:
    def __init__(self, place, sends, buf, rows, cut, send_sem, recv_sem):
        h = rows // 2
        self.place, self.sends, self.buf = place, sends, buf
        self.send_sem, self.recv_sem = send_sem, recv_sem
        right, left, across = (1, 0), (3, 0), (0, 1)
        self.plan = {
            "r1": (right, (0, 0), 0, h),
            "r2": (right, (0, 0), h, rows),
            "r3": (right, (3, 0), 0, h),
            "r4": (right, (0, 1), cut, rows),
            "r5": (right, (3, 1), 0, h),
            "l1": (left, (0, 0), h, rows),
            "l2": (left, (0, 0), 0, h),
            "l3": (left, (1, 0), h, rows),
            "l4": (left, (0, 1), 0, rows - cut),
            "l5": (left, (1, 1), h, rows),
            "z1": (across, (0, 0), 0, h),
            "z2": (across, (0, 0), h, rows),
            "z3": (across, (3, 0), 0, h),
            "z4": (across, (1, 0), h, rows),
            "z5": (across, (3, 0), h, cut),
            "z6": (across, (1, 0), rows - cut, h),
        }
        self.number = {key: i for i, key in enumerate(self.plan)}

    def send(self, *keys):
        for key in keys:
            to, block, first, last = self.plan[key]
            ref = self.buf.at[self.place.block(*block), pl.ds(first, last - first)]
            i = self.number[key]
            self.sends.start(ref, ref, self.send_sem.at[i], self.recv_sem.at[i], self.place.bus_peer(*to))

    def wait(self, *keys):
        for key in keys:
            to, block, first, last = self.plan[key]
            at = self.place.block((block[0] - to[0]) % NX, (block[1] + to[1]) % 2)
            ref = self.buf.at[at, pl.ds(first, last - first)]
            i = self.number[key]
            arrived(ref, self.send_sem.at[i], self.recv_sem.at[i], self.place.bus_peer(*to))

    def begin(self):
        self.send("r1", "l1", "z1", "r2", "l2", "z2")

    def run(self, use):
        block = self.place.block
        use(block(0, 0))
        self.wait("r1")
        self.send("r3", "z3")
        self.wait("l1")
        self.send("l3", "z4")
        self.wait("r2")
        self.send("z5")
        self.wait("l2")
        self.send("z6")
        self.wait("z1")
        self.send("l4")
        self.wait("z2")
        self.send("r4")
        use(block(3, 0))
        self.wait("z3")
        self.send("r5")
        self.wait("z4")
        self.send("l5")
        use(block(1, 0))
        use(block(0, 1))
        self.wait("r3", "l3")
        use(block(2, 0))
        self.wait("z5", "r4")
        use(block(3, 1))
        self.wait("z6", "l4")
        use(block(1, 1))
        self.wait("r5", "l5")
        use(block(2, 1))


class Prefix:
    def __init__(self, place, sends, buf, send_sem, recv_sem):
        self.place, self.sends, self.buf = place, sends, buf
        self.send_sem, self.recv_sem = send_sem, recv_sem

    def begin(self, value):
        place = self.place
        self.buf[place.member] = dot(jnp.ones((ROW, HD), F32), value, ((1,), (1,)), HIGHEST)
        for d in range(1, GROUP):
            ref = self.buf.at[place.member]
            self.sends.start(ref, ref, self.send_sem.at[d - 1], self.recv_sem.at[d - 1], place.member_peer(d))

    def middle(self):
        place = self.place
        for d in range(1, GROUP):
            ref = self.buf.at[lax.rem(place.member - d + GROUP, GROUP)]
            arrived(ref, self.send_sem.at[d - 1], self.recv_sem.at[d - 1], place.member_peer(d))
        total = self.buf[0]
        for i in range(1, GROUP):
            total = total + self.buf[i]
        self.buf[GROUP + place.group] = total
        for d in range(1, GROUP):
            ref = self.buf.at[GROUP + place.group]
            i = GROUP - 2 + d
            self.sends.start(ref, ref, self.send_sem.at[i], self.recv_sem.at[i], place.group_peer(d))

    def end(self, reverse):
        place = self.place
        for d in range(1, GROUP):
            ref = self.buf.at[GROUP + lax.rem(place.group - d + GROUP, GROUP)]
            i = GROUP - 2 + d
            arrived(ref, self.send_sem.at[i], self.recv_sem.at[i], place.group_peer(d))
        count = 2 * GROUP * ROW
        row = lax.broadcasted_iota(jnp.int32, (count, HD), 0)
        slot = row // ROW
        first = lax.rem(row, ROW) == 0
        mine = jnp.where(slot < GROUP, place.member, place.group + GROUP)
        reached = (slot > mine) if reverse else (slot < mine)
        reached = reached & ((slot < GROUP) == (mine < GROUP)) & first
        gathered = self.buf[...].reshape(count, NP)
        return dot(gathered, reached.astype(F32), ((0,), (0,)), HIGHEST)[0:NB]


def kernel(*refs):
    (sens_h, demand_h, cost_h, olim_h, gen_h, llim_h, line_h, sbus_h, clim_h, chg_h, lstart_h, llev_h, ldual_h, bal_h) = refs[:14]
    (gen_o, chg_o, level_o, line_o, ldual_o, bal_o) = refs[14:20]
    (sens, demand, cost, olim_r, gen, llim_r, sbus_r, clim_r, chg, lstart_r, llev_r, ldual, bal, line0) = refs[20:34]
    (shi, slo, tail, lines1, lines2, part1, part2, recv1, recv2, acc, pad_l, pad_c, pad_i, hot, level_v, line_v, pre) = refs[34:51]
    (in_sem, out_sem, g1s, g1r, g2s, g2r, s1s, s1r, s2s, s2r, ps, pr) = refs[51:]
    place = Place()
    sends = Sends()

    ins = {}
    for i, (src, dst) in enumerate(
        (
            (line_h, line0),
            (ldual_h, ldual),
            (sens_h, sens),
            (llim_h, llim_r),
            (sbus_h, sbus_r),
            (olim_h, olim_r),
            (clim_h, clim_r),
            (lstart_h, lstart_r),
            (llev_h, llev_r),
            (bal_h, bal),
            (demand_h, demand),
            (cost_h, cost),
            (gen_h, gen),
            (chg_h, chg),
        )
    ):
        ins[i] = pltpu.make_async_copy(src, dst, in_sem.at[i])
        ins[i].start()

    barrier = pltpu.get_barrier_semaphore()
    partners = [place.bus_peer(*d) for d in PEERS]
    partners += [place.member_peer(d) for d in range(1, GROUP)]
    partners += [place.group_peer(d) for d in range(1, GROUP)]
    for device in partners:
        pl.semaphore_signal(barrier, inc=1, device_id=device, device_id_type=MESH)

    zeros = jnp.zeros((NP - NB, HD), F32)
    for ref in (pad_l, pad_c, pad_i):
        ref[NB:NP, :] = zeros
    acc[...] = jnp.zeros((NP, HD), F32)
    ins[0].wait()
    lines1[place.bus] = line0[...]
    pl.semaphore_wait(barrier, len(partners))

    gather1 = Gather(place, sends, lines1, LD, 256, g1s, g1r)
    gather1.begin()
    prefixes = [Prefix(place, sends, pre.at[k], ps.at[k], pr.at[k]) for k in range(4)]
    ins[1].wait()
    pad_l[0:NB, :] = ldual[...]
    prefixes[0].begin(pad_l[...])

    ins[2].wait()
    tail[0:10, :] = sens[240:NB, :]
    tail[10:16, :] = jnp.zeros((6, NL), F32)

    @pl.loop(0, 15)
    def _(i):
        rows = pl.ds(pl.multiple_of(i * 16, 16), 16)
        shi[rows, :], slo[rows, :] = halves(sens[rows, :])

    shi[240:NP, :], slo[240:NP, :] = halves(tail[...])

    for i in range(3, ARRAYS):
        ins[i].wait()

    def column(row, count):
        return jnp.broadcast_to(row, (HD, count)).T

    olim = column(olim_r[0:1, :], NB)
    clim = column(clim_r[0:1, :], NB)
    lstart = column(lstart_r[0:1, :], NB)
    llev = column(llev_r[0:1, :], NB)
    first_line = pl.multiple_of(place.bus * LD, HD)
    llim = column(llim_r[0:1, pl.ds(first_line, LD)], LD)
    at_bus = lax.broadcasted_iota(jnp.int32, (NP, NB), 0)
    local = sbus_r[0:1, :] - place.bus * NB
    hot[...] = jnp.zeros((NP, NP), F32)
    hot[:, 0:NB] = (at_bus == local).astype(F32)
    hour_at = lax.broadcasted_iota(jnp.int32, (HD, HD), 0)
    hour_to = lax.broadcasted_iota(jnp.int32, (HD, HD), 1)
    until = (hour_at <= hour_to).astype(F32)
    since = (hour_at >= hour_to).astype(F32)
    hour_pos = (place.hour * HD + lax.broadcasted_iota(jnp.int32, (1, HD), 1)).astype(F32)
    step = 1.0 / (float(HOURS) - hour_pos + 4.0)
    prefixes[0].middle()

    def add_adjoint(lines):
        def use(block):
            cols = pl.ds(pl.multiple_of(block * LD, HD), LD)
            high, low = halves(lines[block])
            sh = shi[:, cols]
            acc[...] += dot(sh, high, ((1,), (0,))) + (dot(slo[:, cols], high, ((1,), (0,))) + dot(sh, low, ((1,), (0,))))

        return use

    def flow_part(block, high, low):
        cols = pl.ds(pl.multiple_of(block * LD, HD), LD)
        sh = shi[:, cols]
        return dot(sh, high, ((0,), (0,))) + (dot(slo[:, cols], high, ((0,), (0,))) + dot(sh, low, ((0,), (0,))))

    def primal(balance, later):
        adjoint = acc[0:NB, :]
        at_storage = dot(hot[...], acc[...], ((0,), (0,)), HIGHEST)[0:NB]
        generation, charging = gen[...], chg[...]
        charge_new = jnp.clip(charging - step * (later - at_storage - balance), -clim, clim)
        pad_c[0:NB, :] = 2.0 * charge_new - charging
        output_new = jnp.clip(generation - 0.25 * (cost[...] + adjoint + balance), 0.0, olim)
        gen[...] = output_new
        chg[...] = charge_new
        return 2.0 * output_new - generation - demand[...]

    def flows_begin(output_bar, part, recv, send_sem, recv_sem):
        pad_i[0:NB, :] = output_bar - dot(hot[...], pad_c[...], ((1,), (0,)), HIGHEST)[0:NB]
        injection = pad_i[...]
        high, low = halves(injection)
        total = jnp.broadcast_to(jnp.sum(injection, axis=0, keepdims=True), (ROW, HD))
        for j, (dx, dz) in enumerate(PEERS):
            part[j, 0:LD, :] = flow_part(place.block(dx, dz), high, low)
            part[j, LD : LD + ROW, :] = total
            sends.start(part.at[j], recv.at[j], send_sem.at[j], recv_sem.at[j], place.bus_peer(dx, dz))
        part[7, 0:LD, :] = flow_part(place.bus, high, low)
        part[7, LD : LD + ROW, :] = total

    def flows_end(part, recv, send_sem, recv_sem):
        for j, (dx, dz) in enumerate(PEERS):
            arrived(recv.at[j], send_sem.at[j], recv_sem.at[j], place.bus_peer(dx, dz))
        whole = part[7]
        for j in range(7):
            whole = whole + recv[j]
        return whole[0:LD], whole[LD : LD + 1]

    def line_step(line, flows):
        raised = 4.0 * line + flows
        return 0.25 * (raised - jnp.clip(raised, -llim, llim))

    def level_step(carried):
        level = lstart + carried + dot(pad_c[...], until, ((1,), (0,)), HIGHEST)[0:NB]
        raised = 4.0 * pad_l[0:NB, :] + level
        pad_l[0:NB, :] = 0.25 * (raised - jnp.clip(raised, 0.0, llev))
        return level

    def later_of(carried):
        return carried + dot(pad_l[...], since, ((1,), (0,)), HIGHEST)[0:NB]

    gather1.run(add_adjoint(lines1))
    balance = bal[0:1, :]
    output_bar = primal(balance, later_of(prefixes[0].end(True)))
    prefixes[1].begin(pad_c[...])
    flows_begin(output_bar, part1, recv1, s1s, s1r)
    prefixes[1].middle()
    level_step(prefixes[1].end(False))
    prefixes[2].begin(pad_l[...])
    flows, total = flows_end(part1, recv1, s1s, s1r)
    lines2[place.bus] = line_step(lines1[place.bus], flows)
    gather2 = Gather(place, sends, lines2, LD, 256, g2s, g2r)
    gather2.begin()
    balance = balance + total * (1.0 / float(B + S))
    prefixes[2].middle()

    acc[...] = jnp.zeros((NP, HD), F32)
    gather2.run(add_adjoint(lines2))
    output_bar = primal(balance, later_of(prefixes[2].end(True)))
    prefixes[3].begin(pad_c[...])
    flows_begin(output_bar, part2, recv2, s2s, s2r)
    outs = [pltpu.make_async_copy(gen, gen_o, out_sem.at[0]), pltpu.make_async_copy(chg, chg_o, out_sem.at[1])]
    for copy in outs:
        copy.start()
    prefixes[3].middle()
    level_v[...] = level_step(prefixes[3].end(False))
    ldual[...] = pad_l[0:NB, :]
    more = [pltpu.make_async_copy(level_v, level_o, out_sem.at[2]), pltpu.make_async_copy(ldual, ldual_o, out_sem.at[3])]
    for copy in more:
        copy.start()
    flows, total = flows_end(part2, recv2, s2s, s2r)
    line_v[...] = line_step(lines2[place.bus], flows)
    bal[0:1, :] = balance + total * (1.0 / float(B + S))
    last = [pltpu.make_async_copy(line_v, line_o, out_sem.at[4]), pltpu.make_async_copy(bal, bal_o, out_sem.at[5])]
    for copy in last:
        copy.start()
    for copy in outs + more + last:
        copy.wait()
    sends.finish()


def body(
    line_sensitivity,
    demand,
    unit_cost,
    output_limit,
    output_start,
    line_limit,
    line_dual,
    storage_bus,
    charge_limit,
    charge_start,
    level_start,
    level_limit,
    level_dual,
    balance_dual,
):
    anywhere = pl.BlockSpec(memory_space=pl.ANY)
    block = jax.ShapeDtypeStruct((NB, HD), F32)
    vm = pltpu.VMEM
    dma = pltpu.SemaphoreType.DMA
    scratch = [
        vm((NB, NL), F32),
        vm((NB, HD), F32),
        vm((NB, HD), F32),
        vm((1, NB), F32),
        vm((NB, HD), F32),
        vm((1, NL), F32),
        vm((1, NB), jnp.int32),
        vm((1, NB), F32),
        vm((NB, HD), F32),
        vm((1, NB), F32),
        vm((1, NB), F32),
        vm((NB, HD), F32),
        vm((1, HD), F32),
        vm((LD, HD), F32),
        vm((NP, NL), BF16),
        vm((NP, NL), BF16),
        vm((16, NL), F32),
        vm((8, LD, HD), F32),
        vm((8, LD, HD), F32),
        vm((8, LD + ROW, HD), F32),
        vm((8, LD + ROW, HD), F32),
        vm((7, LD + ROW, HD), F32),
        vm((7, LD + ROW, HD), F32),
        vm((NP, HD), F32),
        vm((NP, HD), F32),
        vm((NP, HD), F32),
        vm((NP, HD), F32),
        vm((NP, NP), F32),
        vm((NB, HD), F32),
        vm((LD, HD), F32),
        vm((4, 2 * GROUP, ROW, NP), F32),
        dma((ARRAYS,)),
        dma((6,)),
        dma((16,)),
        dma((16,)),
        dma((16,)),
        dma((16,)),
        dma((7,)),
        dma((7,)),
        dma((7,)),
        dma((7,)),
        dma((4, 14)),
        dma((4, 14)),
    ]
    generation, charging, level, line, dual, balance = pl.pallas_call(
        kernel,
        out_shape=(block, block, block, jax.ShapeDtypeStruct((LD, HD), F32), block, jax.ShapeDtypeStruct((1, HD), F32)),
        in_specs=[anywhere] * ARRAYS,
        out_specs=[anywhere] * 6,
        scratch_shapes=scratch,
        compiler_params=pltpu.CompilerParams(collective_id=0, has_side_effects=True, vmem_limit_bytes=56 * 1024 * 1024),
    )(
        line_sensitivity,
        demand,
        unit_cost,
        output_limit.reshape(1, NB),
        output_start,
        line_limit.reshape(1, NL),
        line_dual,
        storage_bus.reshape(1, NB),
        charge_limit.reshape(1, NB),
        charge_start,
        level_start.reshape(1, NB),
        level_limit.reshape(1, NB),
        level_dual,
        balance_dual.reshape(1, HD),
    )
    return generation, charging, level, line, dual, balance.reshape(HD)


def solution(mesh):
    both = P("bus", "hour")
    return jax.shard_map(
        body,
        mesh=mesh,
        in_specs=(
            P("bus", None),
            both,
            both,
            P("bus"),
            both,
            P(),
            both,
            P("bus"),
            P("bus"),
            both,
            P("bus"),
            P("bus"),
            both,
            P("hour"),
        ),
        out_specs=(both, both, both, both, both, P("hour")),
        check_vma=False,
    )
```

time: 1490 us -> 109 us (0.07)
  blocking collectives: 1140 us -> 0 us
  local copies, waits for them, and re-layouts: 164 us -> 9 us
  other arithmetic: 112 us -> 0 us
  Pallas kernels: 0 us -> 98 us
  waiting for transfers between devices: 28.1 us -> 0 us
    unnamed x4 -> x0, blocking collectives: 1110 us -> none
    dynamic_slice x258 -> x0, local copies, waits for them, and re-layouts: 137 us -> none  [the longest x256 136 us: hop(): new = combine(before, everything[at])]
    pallas_call x0 -> x1, Pallas kernels: none -> 98 us  [body(): pl.pallas_call(kernel, out_shape=(block, block, block, jax.ShapeDtypeStru...]
    select_n x257 -> x0, other arithmetic: 81.4 us -> none  [the longest x256 81.4 us: hop(): return jnp.where(reached, new, before)]
    psum x2 -> x0, waiting for transfers between devices: 28 us -> none  [flow_update(): flows, balance = lax.psum((partial_value, column_sum), 'bus')]
    psum x2 -> x0, blocking collectives: 27.6 us -> none  [flow_update(): flows, balance = lax.psum((partial_value, column_sum), 'bus')]
  transfers between devices with their start and end apart: 3 -> 0, of which waited for: 1 -> 0; matrix products, arithmetic and copies ran while one was open for 17% -> 0% of each run, Pallas kernels for 0% -> 0%
where the time goes in v1:
time: 109 us; the launch traced here: 108 us
  Pallas kernels  98 us (90%)
  local copies, waits for them, and re-layouts  9 us (8%)
    pallas_call x1, Pallas kernels, body(): pl.pallas_call(kernel, out_shape=(block, block, block, jax.ShapeDtypeStru...  98 us
    unnamed x6, local copies, waits for them, and re-layouts  9 us

profile of v1, /device:TPU:1, one launch (start us, length us, event | category | flops | bytes accessed | tf_op | source)
XLA Modules:
  0.0 107.6 jit_solution(12395884236871574403)
XLA Ops:
  0.6 98.0 %shard_map.181 = (f32[250,128]{1,0:T(8,128)}, f32[250,128]{1,0:T(8,128)}, f32[250,128]{1,0:T(8,128)}, f32[384,128]{1,0:T(8,128)}, f32[250,128]{1,0:T(8,128)}, /*index=5*/f32[1,128]{1,0:T(1,128)}) custom-call(f32[250,3072]{1,0:T(8,128)} %refs_0_.1, f32[250,128]{1,0:T(8,128)} %refs_1_.1, f32[250,128]{1,0:T(8,128)} %refs_2_.1, f32[1,250]{1,0:T(1,128)} %bitcast.9, ...), custom_call_target="tpu_custom_call" | custom-call | tf_op jit(solution)/shard_map/pallas_call | solution.py:451
  98.6 1.6 %copy.26 = f32[250,128]{1,0:T(8,128)} copy(f32[250,128]{1,0:T(8,128)} %get-tuple-element.24) | data formatting | bytes 256000
  100.2 1.6 %copy.27 = f32[250,128]{1,0:T(8,128)} copy(f32[250,128]{1,0:T(8,128)} %get-tuple-element.25) | data formatting | bytes 256000
  101.8 1.6 %copy.28 = f32[250,128]{1,0:T(8,128)} copy(f32[250,128]{1,0:T(8,128)} %get-tuple-element.26) | data formatting | bytes 256000
  103.3 1.6 %copy.29 = f32[384,128]{1,0:T(8,128)} copy(f32[384,128]{1,0:T(8,128)} %get-tuple-element.27) | data formatting | bytes 393216
  104.9 1.6 %copy.30 = f32[250,128]{1,0:T(8,128)} copy(f32[250,128]{1,0:T(8,128)} %get-tuple-element.28) | data formatting | bytes 256000
  106.5 1.1 %copy.31 = f32[128]{0:T(128)} copy(f32[128]{0:T(128)} %bitcast.15) | data formatting | bytes 1024
